TPU v7x, 32 devices: a whole 2x2x4 slice. The times are simulated.
32 devices in a mesh: dp: 4 (over z), expert: 8 (over y, x, core).
Axes of the slice: x: 2, y: 2, z: 4, core: 2. Of those that a mesh axis runs over, the one named last changes fastest.
Arguments:
- tokens: bfloat16 [2048, 2048], P(('dp', 'expert')), may hold values from -6 to 6
- routes: int32 [2048, 4], P(('dp', 'expert')), may hold values from 0 to 59, all different within a row; in each aligned block of 64 rows (0 to 63, 64 to 127, ...) at most 5 rows name the same one
- route_weight: float32 [2048, 4], P(('dp', 'expert')), may hold values from 0.05 to 0.6
- expert_in: bfloat16 [64, 2, 1408, 2048], P('expert', None, 'dp'), may hold values from -0.125 to 0.125
- expert_out: bfloat16 [64, 1408, 2048], P('expert', None, 'dp'), may hold values from -0.15625 to 0.15625
Outputs:
- mixed: bfloat16 [2048, 2048], P(('dp', 'expert'))
Inputs may be any that keep to these rules, and one draw needn't show every extreme that they name: `routes`: within the 64 rows of one device no expert is named by more than 5 rows, and some expert reaches 5 in some device's rows; only experts below 60 are named.
All inputs are finite; a program needn't handle non-finite values.
Results may differ from a plain program's by a relative error of at most 0.0057.
Values may be sent and summed in bfloat16 or wider, within the bound.
A program may use at most 128 MiB of HBM per device.

v0:
```python
import jax
import jax.numpy as jnp
from jax import lax
from jax.sharding import PartitionSpec as P

MOST = 5


def slot_parts(route_rows):
    flat = route_rows.reshape(-1)
    order = jnp.arange(flat.shape[0], dtype=jnp.int32)
    earlier = (flat[:, None] == flat[None, :]) & (order[None, :] < order[:, None])
    return (flat, jnp.sum(earlier.astype(jnp.int32), axis=1))


def pack_rows(source_rows, target, owner, slot_count):
    filled = jnp.zeros((slot_count,), jnp.int32).at[target].set(owner + 1)
    picked = source_rows[jnp.maximum(filled - 1, 0)]
    return jnp.where((filled > 0)[:, None], picked, jnp.zeros_like(picked))


def local(tokens, routes, route_weight, expert_in, expert_out):
    dp_count = lax.axis_size("dp")
    col_count = lax.axis_size("expert")
    local_experts = expert_in.shape[0]
    tok_count = tokens.shape[0]
    route_count = routes.shape[1]
    features = tokens.shape[1]
    slice_width = expert_out.shape[2]
    pair_count = tok_count * route_count
    chosen, rank = slot_parts(routes)
    own_slot = chosen % local_experts * (col_count * MOST) + chosen // local_experts * MOST + rank
    owner = jnp.arange(pair_count, dtype=jnp.int32) // route_count
    packed = pack_rows(tokens, own_slot, owner, local_experts * col_count * MOST)
    packed = packed.reshape(local_experts, col_count, MOST * features)
    arrived = lax.all_to_all(packed, "expert", split_axis=1, concat_axis=1, tiled=True)
    arrived = arrived.reshape(local_experts, col_count * MOST, features)
    both = jnp.einsum(
        "erd,egfd->gefr",
        lax.all_gather(arrived, "dp", axis=1, tiled=True),
        expert_in,
        preferred_element_type=jnp.float32,
    )
    hidden = (jax.nn.silu(both[0]) * both[1]).astype(jnp.bfloat16)
    piece = lax.all_gather(hidden, "dp", axis=1, tiled=True)
    width = piece.shape[1]
    blocks = piece.reshape(local_experts, width, dp_count, col_count, MOST)
    outputs = jnp.einsum(
        "efabm,efd->ebmad", blocks, expert_out, preferred_element_type=jnp.float32
    ).astype(jnp.bfloat16)
    outputs = outputs.reshape(local_experts, col_count, MOST, dp_count * slice_width)
    returned = lax.all_to_all(
        lax.all_to_all(outputs, "dp", split_axis=3, concat_axis=3, tiled=True),
        "expert",
        split_axis=1,
        concat_axis=1,
        tiled=True,
    )
    returned = returned.reshape(local_experts * col_count * MOST, features)
    picked = returned[own_slot].reshape(tok_count, route_count, features)
    mixed = jnp.sum(route_weight[:, :, None] * picked.astype(jnp.float32), axis=1)
    return mixed.astype(jnp.bfloat16)


def solution(mesh):
    return jax.shard_map(
        local,
        mesh=mesh,
        in_specs=(
            P(("dp", "expert"), None),
            P(("dp", "expert"), None),
            P(("dp", "expert"), None),
            P("expert", None, "dp", None),
            P("expert", None, "dp"),
        ),
        out_specs=P(("dp", "expert"), None),
        check_vma=False,
    )
```

profile of v0, /device:TPU:25, one launch (start us, length us, event | category | flops | bytes accessed | tf_op | source)
XLA Modules:
  0.0 444.9 jit_solution(1361350592039279218)
XLA Ops:
  6.5 0.0 copy-start
  6.5 0.0 all-gather.3.cloned.1.call-start
  6.5 0.8 copy.47
  7.4 0.1 eq.17
  7.5 0.1 reshape.147
  7.6 0.2 convert_reduce_fusion
  7.8 1.4 scatter_custom_fusion
  9.2 0.0 copy-done
  9.2 2.4 gather_fusion
  11.7 1.3 gather.9
  13.0 0.1 broadcast_in_dim.24
  13.2 0.1 copy.49
  13.3 0.2 broadcast_in_dim.25
  13.6 1.5 copy_select_fusion
  15.1 21.0 %all_to_all.15 = bf16[8,8,10240]{2,0,1:T(8,128)(2,1)S(1)} all-to-all(bf16[8,8,10240]{2,0,1:T(8,128)(2,1)S(1)} %copy_select_fusion), channel_id=1, replica_groups=mesh['dp'=4,'expert'=8] {'expert'}, dimensions={1} | all-to-all | bytes 2621440 | tf_op jit(solution)/shard_map/all_to_all | solution.py:36
  36.2 0.7 copy.51
  36.9 2.2 reshape.148
  39.1 0.0 all-gather.3.cloned.1.call-update
  39.1 0.2 all-gather.5.cloned.1.call-start
  39.3 95.1 %all-gather.3.cloned.1.call-done = bf16[8,160,2048]{2,1,0:T(8,128)(2,1)} async-done(((bf16[8,40,2048]{2,1,0:T(8,128)(2,1)}), bf16[8,160,2048]{2,1,0:T(8,128)(2,1)}) %all-gather.3.cloned.1.call-update) | async-done | bytes 5242896 | tf_op jit(solution)/shard_map/all_gather | solution.py:40
  134.4 15.0 %fusion.5 = f32[2,8,352,160]{2,3,0,1:T(8,128)} fusion(bf16[8,2,352,2048]{3,2,1,0:T(8,128)(2,1)} %param.8, bf16[8,160,2048]{2,1,0:T(8,128)(2,1)} %all-gather.3.cloned.1.call-done), kind=kOutput, calls=%fused_computation.9 | convolution fusion | flops 3690987520 | bytes 31916032 | tf_op jit(solution)/shard_map/erd,egfd->gefr/dot_general | solution.py:38
  149.4 2.7 fusion.9
  152.0 2.0 copy.53
  154.0 0.0 all-gather.5.cloned.1.call-update
  154.0 105.1 %all-gather.5.cloned.1.call-done = bf16[8,1408,160]{2,0,1:T(8,128)(2,1)} async-done(((bf16[8,352,160]{2,0,1:T(8,128)(2,1)}), bf16[8,1408,160]{2,0,1:T(8,128)(2,1)}) %all-gather.5.cloned.1.call-update) | async-done | bytes 3604496 | tf_op jit(solution)/shard_map/all_gather | solution.py:45
  259.2 9.2 %copy.54 = bf16[8,1408,160]{1,0,2:T(8,128)(2,1)} copy(bf16[8,1408,160]{2,0,1:T(8,128)(2,1)} %all-gather.5.cloned.1.call-done) | data formatting | bytes 7208960 | tf_op jit(solution)/shard_map/all_gather | solution.py:45
  268.4 7.6 %fusion.15 = bf16[8,8,5,4,512]{4,1,2,3,0:T(8,128)(2,1)S(1)} fusion(bf16[8,1408,512]{2,1,0:T(8,128)(2,1)} %param.9, bf16[8,1408,4,8,5]{1,0,4,3,2:T(8,128)(2,1)} %bitcast.42), kind=kOutput, calls=%fused_computation.15 | convolution fusion | flops 1846149120 | bytes 16449536 | tf_op jit(solution)/shard_map/efabm,efd->ebmad/dot_general | solution.py:48
  275.9 13.8 %copy.62 = bf16[8,8,5,4,512]{1,0,2,4,3:T(8,128)(2,1)} copy(bf16[8,8,5,4,512]{4,1,2,3,0:T(8,128)(2,1)S(1)} %fusion.15) | data formatting | bytes 2621440 | tf_op jit(solution)/shard_map/reshape | solution.py:51
  289.8 32.9 %reshape.182 = bf16[4,2,81920]{2,1,0:T(2,128)(2,1)S(1)} reshape(bf16[2048,5,8,8]{3,2,1,0:T(8,128)(2,1)} %bitcast.40) | data formatting | bytes 2621440
  322.6 34.8 %all_to_all.16 = bf16[4,2,81920]{2,1,0:T(2,128)(2,1)S(1)} all-to-all(bf16[4,2,81920]{2,1,0:T(2,128)(2,1)S(1)} %reshape.182), channel_id=1, replica_groups=mesh['dp'=4,'expert'=8] {'dp'}, dimensions={0} | all-to-all | bytes 2621440 | tf_op jit(solution)/shard_map/all_to_all | solution.py:53
  357.4 33.3 %reshape.183 = bf16[2048,5,8,8]{3,2,1,0:T(8,128)(2,1)} reshape(bf16[4,2,81920]{2,1,0:T(2,128)(2,1)S(1)} %all_to_all.16) | data formatting | bytes 2621440
  390.7 18.9 %copy.58 = bf16[8,8,5,2048]{3,0,2,1:T(8,128)(2,1)} copy(bf16[8,8,5,2048]{1,0,2,3:T(8,128)(2,1)} %bitcast.41) | data formatting | bytes 2621440 | tf_op jit(solution)/shard_map/all_to_all | solution.py:53
  409.5 0.0 copy-start.2
  409.5 4.8 %all-to-all-start.2 = ((bf16[8,8,5,2048]{3,0,2,1:T(8,128)(2,1)}), bf16[8,8,5,2048]{3,0,2,1:T(8,128)(2,1)S(1)}, u32[]{:S(2)}, u32[]{:S(2)}) async-start(bf16[8,8,5,2048]{3,0,2,1:T(8,128)(2,1)} %copy.58), calls=%async_computation.2 | async-start | bytes 2621440 | tf_op jit(solution)/shard_map/all_to_all | solution.py:52
  414.4 0.0 copy-done.2
  414.4 0.1 copy.46
  414.5 14.5 %all-to-all-done.2 = bf16[8,8,5,2048]{3,0,2,1:T(8,128)(2,1)S(1)} async-done(((bf16[8,8,5,2048]{3,0,2,1:T(8,128)(2,1)}), bf16[8,8,5,2048]{3,0,2,1:T(8,128)(2,1)S(1)}, u32[]{:S(2)}, u32[]{:S(2)}) %all-to-all-start.2) | async-done | bytes 1310752 | tf_op jit(solution)/shard_map/all_to_all | solution.py:52
  429.0 2.1 copy.59
  431.1 2.6 reshape.151
  433.7 1.4 gather_fusion.1
  435.0 0.0 copy-start.1
  435.0 0.7 reshape.152
  435.8 2.3 multiply_reduce_fusion
  438.0 0.0 copy-done.1
  (6 shorter events, 0.0 us)
Async XLA Ops:
  6.5 2.7 copy-start
  6.5 127.9 %all-gather.3.cloned.1.call-start = ((), (), s32[]{:S(2)}) async-start(), calls=%async_computation.3 | async-start | bytes 6553600 | tf_op jit(solution)/shard_map/all_gather | solution.py:40
  39.1 220.1 %all-gather.5.cloned.1.call-start = ((), (), s32[]{:S(2)}) async-start(), calls=%async_computation.4 | async-start | bytes 7208960 | tf_op jit(solution)/shard_map/all_gather | solution.py:45
  409.5 4.9 %copy-start.2 = (f32[64,4]{0,1:T(4,128)S(1)}, f32[64,4]{0,1:T(4,128)}, u32[]{:S(2)}) copy-start(f32[64,4]{0,1:T(4,128)} %param.7) | copy-start | bytes 3076
  409.5 19.5 %all-to-all-start.2 = ((bf16[8,8,5,2048]{3,0,2,1:T(8,128)(2,1)}), bf16[8,8,5,2048]{3,0,2,1:T(8,128)(2,1)S(1)}, u32[]{:S(2)}, u32[]{:S(2)}) async-start(bf16[8,8,5,2048]{3,0,2,1:T(8,128)(2,1)} %copy.58), calls=%async_computation.2 | async-start | bytes 2621440 | tf_op jit(solution)/shard_map/all_to_all | solution.py:52
  435.0 3.0 copy-start.1
Sparse Core Ops, SparseCore 0:
  39.2 95.1 all-gather.2
  154.2 104.9 all-gather.4
where the time goes:
time: 452 us; the launch traced here: 445 us
  waiting for transfers between devices  215 us (48%)
  local copies, waits for them, and re-layouts  126 us (28%)
  blocking collectives  55.8 us (12%)
  matrix products  22.5 us (5%)
  between operations  13.5 us (3%)
  other arithmetic  6.72 us (1%)
  starting transfers between devices  5.07 us (1%)
    all_gather x1, waiting for transfers between devices, local(): piece = lax.all_gather(hidden, 'dp', axis=1, tiled=True)  105 us
    all_gather x1, waiting for transfers between devices, local(): lax.all_gather(arrived, 'dp', axis=1, tiled=True)  95.1 us
    unnamed x10, local copies, waits for them, and re-layouts  67.1 us
    all_to_all x1, blocking collectives, local(): lax.all_to_all(outputs, 'dp', split_axis=3, concat_axis=3, tiled=True)  34.8 us
    all_to_all x1, blocking collectives, local(): lax.all_to_all(packed, 'expert', split_axis=1, concat_axis=1, tiled=True)  21 us
    all_to_all x1, local copies, waits for them, and re-layouts, local(): lax.all_to_all(outputs, 'dp', split_axis=3, concat_axis=3, tiled=True)  18.9 us
    dot_general x1, matrix products, local(): jnp.einsum('erd,egfd->gefr', lax.all_gather(arrived, 'dp', axis=1, tiled=...  15 us
    all_to_all x1, waiting for transfers between devices, local(): lax.all_to_all(lax.all_to_all(outputs, 'dp', split_axis=3, concat_axis=3,...  14.5 us
  transfers between devices with their start and end apart: 3, of which 3 were waited for; matrix products, arithmetic and copies ran while one was open for 0% of the time, Pallas kernels for 0%

commit v1 on v0

--- a/solution.py
+++ b/solution.py
@@ -1,9 +1,15 @@
+import functools
+
 import jax
 import jax.numpy as jnp
 from jax import lax
+from jax.experimental import pallas as pl
+from jax.experimental.pallas import tpu as pltpu
 from jax.sharding import PartitionSpec as P
 
 MOST = 5
+META = 128
+MESH = pl.DeviceIdType.MESH
 
 
 def slot_parts(route_rows):
@@ -62,9 +68,343 @@
     return mixed.astype(jnp.bfloat16)
 
 
+def gather_kernel(n, cols, own_ref, out_ref, own_sem, send_sem, recv_sem):
+    z, c = lax.axis_index("dp"), lax.axis_index("expert")
+    sib_of = lambda col: col + 1 - 2 * (col % 2)
+    xn = c + 2 - 4 * ((c // 2) % 2)
+    yn = c + 4 - 8 * (c // 4)
+    diag = xn + 4 - 8 * (xn // 4)
+    sib = sib_of(c)
+    half = own_ref.shape[0] // 2
+
+    barrier = pltpu.get_barrier_semaphore()
+    for col in (xn, yn, sib):
+        pl.semaphore_signal(barrier, inc=1, device_id=(z, col), device_id_type=MESH)
+
+    @pl.when(z > 0)
+    def _():
+        pl.semaphore_signal(barrier, inc=1, device_id=(z - 1, c), device_id_type=MESH)
+
+    @pl.when(z < n - 1)
+    def _():
+        pl.semaphore_signal(barrier, inc=1, device_id=(z + 1, c), device_id_type=MESH)
+
+    own = pltpu.make_async_copy(own_ref, out_ref.at[z * cols + c], own_sem)
+    own.start()
+    own.wait()
+    pl.semaphore_wait(barrier, 3 + (z > 0).astype(jnp.int32) + (z < n - 1).astype(jnp.int32))
+
+    def copy(block, kind, target, part=None):
+        if part is None:
+            ref, sem = out_ref.at[block], recv_sem.at[block, 0]
+        else:
+            ref, sem = out_ref.at[block, pl.ds(part * half, half)], recv_sem.at[block, part]
+        return pltpu.make_async_remote_copy(
+            src_ref=ref, dst_ref=ref, send_sem=send_sem.at[block, kind], recv_sem=sem,
+            device_id=target, device_id_type=MESH,
+        )
+
+    def along_z(off, go):
+        zz = z + off
+        block = zz * cols + c
+        if off <= 0:
+            @pl.when(z < n - 1)
+            def _():
+                go(copy(block, 0, (z + 1, c)))
+        if off >= 0:
+            @pl.when(z > 0)
+            def _():
+                go(copy(block, 1, (z - 1, c)))
+        go(copy(block, 2, (z, xn)))
+        go(copy(block, 3, (z, yn)))
+        go(copy(block, 4, (z, sib)))
+
+    def in_plane(off, go, wait):
+        bx, by = (z + off) * cols + xn, (z + off) * cols + yn
+        if wait:
+            copy(bx, 0, (z, xn)).wait_recv()
+        go(copy(bx, 0, (z, yn), 0))
+        go(copy(bx, 4, (z, sib)))
+        if wait:
+            copy(by, 0, (z, yn)).wait_recv()
+        go(copy(by, 0, (z, xn), 1))
+        go(copy(by, 4, (z, sib)))
+
+    def across(off, go, wait):
+        bd = (z + off) * cols + diag
+        if wait:
+            copy(bd, 0, (z, yn), 0).wait_recv()
+            copy(bd, 1, (z, xn), 1).wait_recv()
+        go(copy(bd, 4, (z, sib)))
+
+    offs = [0]
+    for d in range(1, n):
+        offs += [-d, d]
+    start = lambda cp: cp.start()
+
+    def on_slice(off, f):
+        if off == 0:
+            f()
+        elif off < 0:
+            pl.when(z + off >= 0)(f)
+        else:
+            pl.when(z + off < n)(f)
+
+    for i in range(len(offs) + 2):
+        if i < len(offs):
+            def first(off=offs[i]):
+                if off != 0:
+                    copy((z + off) * cols + c, 0, (z, sib)).wait_recv()
+                along_z(off, start)
+            on_slice(offs[i], first)
+        if 0 <= i - 1 < len(offs):
+            on_slice(offs[i - 1], functools.partial(in_plane, offs[i - 1], start, True))
+        if i >= 2:
+            on_slice(offs[i - 2], functools.partial(across, offs[i - 2], start, True))
+
+    sent = lambda cp: cp.wait_send()
+    for off in offs:
+        def last(off=off):
+            for col in (c, xn, yn, diag):
+                copy((z + off) * cols + sib_of(col), 0, (z, sib)).wait_recv()
+            along_z(off, sent)
+            in_plane(off, sent, False)
+            across(off, sent, False)
+        on_slice(off, last)
+
+
+def expert_kernel(
+    n, cols, x_ref, win_ref, wout_ref, perm_ref, weight_ref, out_ref,
+    win, wout, hid, outs, msg, got, win_sem, wout_sem, hid_send, hid_recv, msg_send, msg_recv,
+):
+    z, c = lax.axis_index("dp"), lax.axis_index("expert")
+    me = z * cols + c
+    total = n * cols
+    experts, rows = win.shape[0], hid.shape[2]
+    features = win.shape[3]
+    width = outs.shape[1]
+
+    @pl.loop(0, experts)
+    def _(e):
+        pltpu.make_async_copy(win_ref.at[e], win.at[e], win_sem.at[e]).start()
+
+    @pl.loop(0, experts)
+    def _(e):
+        pltpu.make_async_copy(wout_ref.at[e], wout.at[e], wout_sem.at[e]).start()
+
+    barrier = pltpu.get_barrier_semaphore()
+
+    @pl.loop(1, total)
+    def _(d):
+        other = (me + d) % total
+        pl.semaphore_signal(barrier, inc=1, device_id=(other // cols, other % cols), device_id_type=MESH)
+
+    pl.semaphore_wait(barrier, total - 1)
+
+    def pass_on(zz, e, way, target):
+        return pltpu.make_async_remote_copy(
+            src_ref=hid.at[zz, e], dst_ref=hid.at[zz, e], send_sem=hid_send.at[zz, e, way],
+            recv_sem=hid_recv.at[zz, e], device_id=(target, c), device_id_type=MESH,
+        )
+
+    def upward(zz, e):
+        @pl.when(z < n - 1)
+        def _():
+            pass_on(zz, e, 0, z + 1).start()
+
+    def downward(zz, e):
+        @pl.when(z > 0)
+        def _():
+            pass_on(zz, e, 1, z - 1).start()
+
+    contract_last = (((1,), (1,)), ((), ()))
+
+    @pl.loop(0, experts + n - 1)
+    def _(i):
+        @pl.when(i < experts)
+        def _():
+            pltpu.make_async_copy(win_ref.at[i], win.at[i], win_sem.at[i]).wait()
+            x = x_ref[:, i, :, :features].reshape(rows, features)
+            gate = lax.dot_general(x, win[i, 0], contract_last, preferred_element_type=jnp.float32)
+            up = lax.dot_general(x, win[i, 1], contract_last, preferred_element_type=jnp.float32)
+            hid[z, i] = (gate / (1.0 + jnp.exp(-gate)) * up).astype(jnp.bfloat16)
+            upward(z, i)
+            downward(z, i)
+
+        for d in range(1, n):
+            e = i - d
+
+            @pl.when((e >= 0) & (e < experts) & (z - d >= 0))
+            def _():
+                pass_on(z - d, e, 0, (z + 1) % n).wait_recv()
+                upward(z - d, e)
+
+            @pl.when((e >= 0) & (e < experts) & (z + d < n))
+            def _():
+                pass_on(z + d, e, 1, (z + 1) % n).wait_recv()
+                downward(z + d, e)
+
+        @pl.when(i >= n - 1)
+        def _():
+            e = i - (n - 1)
+            pltpu.make_async_copy(wout_ref.at[e], wout.at[e], wout_sem.at[e]).wait()
+            acc = jnp.zeros((rows, width), jnp.float32)
+            for zz in range(n):
+                acc += jnp.dot(hid[zz, e], wout[e, zz], preferred_element_type=jnp.float32)
+            outs[pl.ds(pl.multiple_of(e * rows, rows), rows), :] = acc.astype(jnp.bfloat16)
+
+    def message(dest):
+        return pltpu.make_async_remote_copy(
+            src_ref=msg.at[dest], dst_ref=got.at[me], send_sem=msg_send.at[dest],
+            recv_sem=msg_recv.at[me], device_id=(dest // cols, dest % cols), device_id_type=MESH,
+        )
+
+    slots = msg.shape[1]
+
+    @pl.loop(0, n)
+    def _(j):
+        zz = (z + 1 + j) % n
+        part = perm_ref[pl.ds(pl.multiple_of(zz * (cols * slots), cols * slots), cols * slots), :]
+        lanes = lax.broadcasted_iota(jnp.int32, (cols * slots, outs.shape[0]), 1)
+        pick = jnp.where(lanes == part, 1.0, 0.0).astype(jnp.bfloat16)
+        moved = jnp.dot(pick, outs[...], preferred_element_type=jnp.float32)
+        msg[pl.ds(zz * cols, cols)] = moved.reshape(cols, slots, width).astype(jnp.bfloat16)
+
+        @pl.loop(0, cols)
+        def _(k):
+            dest = zz * cols + (c + k) % cols
+
+            @pl.when(dest != me)
+            def _():
+                message(dest).start()
+
+    got[me] = msg[me]
+
+    @pl.loop(1, total)
+    def _(d):
+        source = (me + d) % total
+        pltpu.make_async_remote_copy(
+            src_ref=msg.at[source], dst_ref=got.at[source], send_sem=msg_send.at[source],
+            recv_sem=msg_recv.at[source], device_id=(source // cols, source % cols), device_id_type=MESH,
+        ).wait_recv()
+
+    tok = out_ref.shape[0]
+    for zz in range(n):
+        acc = jnp.zeros((2 * tok, width), jnp.float32)
+        for col in range(cols):
+            acc += jnp.dot(weight_ref[col], got[zz * cols + col], preferred_element_type=jnp.float32)
+        out_ref[:, zz * width:(zz + 1) * width] = (acc[:tok] + acc[tok:]).astype(jnp.bfloat16)
+
+    @pl.loop(1, total)
+    def _(d):
+        message((me + d) % total).wait_send()
+
+    @pl.loop(0, experts)
+    def _(e):
+        for zz in range(n):
+            @pl.when((z < n - 1) & (zz <= z))
+            def _():
+                pass_on(zz, e, 0, z + 1).wait_send()
+
+            @pl.when((z > 0) & (zz >= z))
+            def _():
+                pass_on(zz, e, 1, z - 1).wait_send()
+
+
+def fused(n, cols, tokens, routes, route_weight, expert_in, expert_out):
+    tok, features = tokens.shape
+    top = routes.shape[1]
+    experts, _, hidden, _ = expert_in.shape
+    width = expert_out.shape[2]
+    total = n * cols
+    col = lax.axis_index("expert")
+    slots = experts * MOST
+    rows = total * MOST
+
+    chosen, rank = slot_parts(routes)
+    rank = rank.reshape(tok, top)
+    meta = jnp.concatenate([routes, rank, jnp.zeros((tok, META - 2 * top), jnp.int32)], axis=1)
+    block = jnp.concatenate([tokens, meta.astype(jnp.bfloat16)], axis=1)
+    gathered = pl.pallas_call(
+        functools.partial(gather_kernel, n, cols),
+        out_shape=jax.ShapeDtypeStruct((total, tok, features + META), jnp.bfloat16),
+        in_specs=[pl.BlockSpec(memory_space=pl.ANY)],
+        out_specs=pl.BlockSpec(memory_space=pl.ANY),
+        scratch_shapes=[
+            pltpu.SemaphoreType.DMA,
+            pltpu.SemaphoreType.DMA((total, 5)),
+            pltpu.SemaphoreType.DMA((total, 2)),
+        ],
+        compiler_params=pltpu.CompilerParams(collective_id=0, has_side_effects=True),
+    )(block)
+
+    groups = 2
+    per_group = rows // groups
+    seen = gathered[:, :, features:features + 2 * top].astype(jnp.int32)
+    expert = col * experts + jnp.arange(experts, dtype=jnp.int32)
+    base = (jnp.arange(total, dtype=jnp.int32) % (total // groups)) * MOST
+    slot = seen[:, :, top:] + base[:, None, None] + 1
+    match = seen[None, :, :, :top] == expert[:, None, None, None]
+    place = jnp.sum(jnp.where(match, slot[None], 0), axis=3) - 1
+    place = place.reshape(experts, groups, total // groups * tok).transpose(1, 0, 2)
+    pick = place[:, :, None, :] == jnp.arange(per_group, dtype=jnp.int32)[None, None, :, None]
+    x = jnp.einsum(
+        "gst,gtd->gsd",
+        pick.astype(jnp.bfloat16).reshape(groups, experts * per_group, -1),
+        gathered.reshape(groups, total // groups * tok, features + META),
+        preferred_element_type=jnp.bfloat16,
+    ).reshape(groups, experts, per_group, features + META)
+
+    order = jnp.arange(total * slots, dtype=jnp.int32)
+    perm = (order % slots // MOST * rows + order // slots * MOST + order % MOST)[:, None]
+    spot = (chosen * MOST).reshape(tok, top) + rank
+    exact = jnp.sum(
+        jnp.where(
+            spot[:, :, None] == jnp.arange(cols * slots, dtype=jnp.int32), route_weight[:, :, None], 0.0
+        ),
+        axis=1,
+    )
+    high = lax.reduce_precision(exact, 8, 7)
+    weight = jnp.concatenate([high, exact - high], axis=0).astype(jnp.bfloat16)
+    weight = weight.reshape(2 * tok, cols, slots).transpose(1, 0, 2)
+
+    vmem = pl.BlockSpec(memory_space=pltpu.VMEM)
+    anywhere = pl.BlockSpec(memory_space=pl.ANY)
+    return pl.pallas_call(
+        functools.partial(expert_kernel, n, cols),
+        out_shape=jax.ShapeDtypeStruct((tok, features), jnp.bfloat16),
+        in_specs=[vmem, anywhere, anywhere, vmem, vmem],
+        out_specs=vmem,
+        scratch_shapes=[
+            pltpu.VMEM((experts, 2, hidden, features), jnp.bfloat16),
+            pltpu.VMEM((experts, n, hidden, width), jnp.bfloat16),
+            pltpu.VMEM((n, experts, rows, hidden), jnp.bfloat16),
+            pltpu.VMEM((experts * rows, width), jnp.bfloat16),
+            pltpu.VMEM((total, slots, width), jnp.bfloat16),
+            pltpu.VMEM((total, slots, width), jnp.bfloat16),
+            pltpu.SemaphoreType.DMA((experts,)),
+            pltpu.SemaphoreType.DMA((experts,)),
+            pltpu.SemaphoreType.DMA((n, experts, 2)),
+            pltpu.SemaphoreType.DMA((n, experts)),
+            pltpu.SemaphoreType.DMA((total,)),
+            pltpu.SemaphoreType.DMA((total,)),
+        ],
+        compiler_params=pltpu.CompilerParams(
+            collective_id=1, has_side_effects=True, vmem_limit_bytes=60 * 1024 * 1024
+        ),
+    )(x, expert_in, expert_out.reshape(experts, n, hidden, width), perm, weight)
+
+
 def solution(mesh):
+    n, cols = mesh.shape["dp"], mesh.shape["expert"]
+
+    def body(*args):
+        if n * cols > 32 or cols != 8:
+            return local(*args)
+        return fused(n, cols, *args)
+
     return jax.shard_map(
-        local,
+        body,
         mesh=mesh,
         in_specs=(
             P(("dp", "expert"), None),

time: 452 us -> 191 us (0.42); the launches traced: 445 us -> 190 us
  waiting for transfers between devices: 215 us -> 0 us
  Pallas kernels: 0 us -> 166 us
  local copies, waits for them, and re-layouts: 126 us -> 6.55 us
  blocking collectives: 55.8 us -> 0 us
  between operations: 13.5 us -> 0.13 us
  matrix products: 22.5 us -> 11.6 us
  starting transfers between devices: 5.07 us -> 0 us
    all_gather x2 -> x0, waiting for transfers between devices: 200 us -> none  [the longest x1 105 us: local(): piece = lax.all_gather(hidden, 'dp', axis=1, tiled=True)]
    pallas_call x0 -> x2, Pallas kernels: none -> 166 us  [the longest x1 111 us: fused(): pl.pallas_call(functools.partial(expert_kernel, n, cols), out_shape=jax.S...]
    unnamed x10 -> x4, local copies, waits for them, and re-layouts: 67.1 us -> 2.45 us
    all_to_all x2 -> x0, blocking collectives: 55.8 us -> none  [the longest x1 34.8 us: local(): lax.all_to_all(outputs, 'dp', split_axis=3, concat_axis=3, tiled=True)]
    all_to_all x3 -> x0, local copies, waits for them, and re-layouts: 21.7 us -> none  [the longest x1 18.9 us: local(): lax.all_to_all(outputs, 'dp', split_axis=3, concat_axis=3, tiled=True)]
    reshape x4 -> x2, local copies, waits for them, and re-layouts: 18.7 us -> 0.18 us  [fused(): rank = rank.reshape(tok, top)]
    all_to_all x1 -> x0, waiting for transfers between devices: 14.5 us -> none  [local(): lax.all_to_all(lax.all_to_all(outputs, 'dp', split_axis=3, concat_axis=3,...]
    dot_general x2 -> x1, matrix products: 22.5 us -> 11.6 us  [fused(): jnp.einsum('gst,gtd->gsd', pick.astype(jnp.bfloat16).reshape(groups, expe...]
  transfers between devices with their start and end apart: 3 -> 0, of which waited for: 3 -> 0; matrix products, arithmetic and copies ran while one was open for 0% -> 0% of each run, Pallas kernels for 0% -> 0%
where the time goes in v1:
time: 191 us; the launch traced here: 190 us
  Pallas kernels  166 us (87%)
  matrix products  11.6 us (6%)
  local copies, waits for them, and re-layouts  6.55 us (3%)
  other arithmetic  5.91 us (3%)
    pallas_call x1, Pallas kernels, fused(): pl.pallas_call(functools.partial(expert_kernel, n, cols), out_shape=jax.S...  111 us
    pallas_call x1, Pallas kernels, fused(): pl.pallas_call(functools.partial(gather_kernel, n, cols), out_shape=jax.S...  54.7 us
    dot_general x1, matrix products, fused(): jnp.einsum('gst,gtd->gsd', pick.astype(jnp.bfloat16).reshape(groups, expe...  11.6 us

profile of v1, /device:TPU:25, one launch (start us, length us, event | category | flops | bytes accessed | tf_op | source)
XLA Modules:
  0.0 189.7 jit_solution(8070612530901386795)
XLA Ops:
  0.0 0.8 copy.35
  0.8 0.1 eq.66
  0.9 0.2 convert_reduce_fusion
  1.1 0.1 reshape.150
  1.2 0.1 copy.41
  1.3 0.8 multiply_add_fusion
  2.0 0.1 copy.36
  2.2 1.8 concatenate.11.own_ref
  3.9 54.7 %shard_map.55 = bf16[32,64,2176]{2,1,0:T(8,128)(2,1)} custom-call(bf16[64,2176]{1,0:T(8,128)(2,1)} %concatenate.11.own_ref), custom_call_target="tpu_custom_call" | custom-call | tf_op jit(solution)/shard_map/pallas_call | solution.py:328
  58.7 1.1 slice_convert_fusion
  59.8 0.5 fusion.26
  60.3 0.4 copy.37
  60.7 0.4 copy.39
  61.1 0.1 select_reduce_fusion
  61.3 0.1 sub.21
  61.4 0.1 eq.76
  61.5 0.8 bitcast_compare_fusion
  62.3 0.0 copy-start
  62.3 11.6 %fusion.27 = bf16[2,640,2176]{2,1,0:T(8,128)(2,1)} fusion(pred[2,640,1024]{2,1,0:T(32,128)(4,1)S(1)} %bitcast_compare_fusion, bf16[2,1024,2176]{2,1,0:T(8,128)(2,1)} %bitcast.11), kind=kOutput, calls=%fused_computation.48 | convolution fusion | flops 5704253440 | bytes 15794176 | tf_op jit(solution)/shard_map/gst,gtd->gsd/dot_general | solution.py:351
  73.9 0.0 copy-done
  73.9 0.1 select_reduce_fusion.1
  74.0 0.1 copy.42
  74.2 0.1 pad_maximum_fusion
  74.3 0.9 copy.43
  75.1 2.1 %fusion.13.perm_ref = s32[1280,1]{1,0:T(8,128)} fusion(), kind=kLoop, calls=%fused_computation.21 | loop fusion | flops 38400 | bytes 5120 | tf_op jit(solution)/shard_map/add | solution.py:359
  77.2 110.8 %shard_map.56 = bf16[64,2048]{1,0:T(8,128)(2,1)} custom-call(bf16[2,8,80,2176]{3,2,1,0:T(8,128)(2,1)} %bitcast.10, bf16[8,2,352,2048]{3,2,1,0:T(8,128)(2,1)} %win_ref.1, bf16[8,4,352,512]{3,2,1,0:T(8,128)(2,1)} %bitcast.12, s32[1280,1]{1,0:T(8,128)} %fusion.13.perm_ref, bf16[8,128,40]{2,1,0:T(8,128)(2,1)} %bitcast.13), custom_call_target="tpu_custom_call" | custom-call | tf_op jit(solution)/shard_map/pallas_call | solution.py:373
  188.1 1.7 copy.47
  (8 shorter events, 0.1 us)
Async XLA Ops:
  62.3 11.6 %copy-start = (f32[64,4]{0,1:T(4,128)S(1)}, f32[64,4]{0,1:T(4,128)}, u32[]{:S(2)}) copy-start(f32[64,4]{0,1:T(4,128)} %param.7) | copy-start | bytes 3076

commit v2 on v1

v2 whole, which is shorter than its diff:
```python
import functools

import jax
import jax.numpy as jnp
from jax import lax
from jax.experimental import pallas as pl
from jax.experimental.pallas import tpu as pltpu
from jax.sharding import PartitionSpec as P

MOST = 5
MESH = pl.DeviceIdType.MESH


def slot_parts(route_rows):
    flat = route_rows.reshape(-1)
    order = jnp.arange(flat.shape[0], dtype=jnp.int32)
    earlier = (flat[:, None] == flat[None, :]) & (order[None, :] < order[:, None])
    return (flat, jnp.sum(earlier.astype(jnp.int32), axis=1))


def pack_rows(source_rows, target, owner, slot_count):
    filled = jnp.zeros((slot_count,), jnp.int32).at[target].set(owner + 1)
    picked = source_rows[jnp.maximum(filled - 1, 0)]
    return jnp.where((filled > 0)[:, None], picked, jnp.zeros_like(picked))


def local(tokens, routes, route_weight, expert_in, expert_out):
    dp_count = lax.axis_size("dp")
    col_count = lax.axis_size("expert")
    local_experts = expert_in.shape[0]
    tok_count = tokens.shape[0]
    route_count = routes.shape[1]
    features = tokens.shape[1]
    slice_width = expert_out.shape[2]
    pair_count = tok_count * route_count
    chosen, rank = slot_parts(routes)
    own_slot = chosen % local_experts * (col_count * MOST) + chosen // local_experts * MOST + rank
    owner = jnp.arange(pair_count, dtype=jnp.int32) // route_count
    packed = pack_rows(tokens, own_slot, owner, local_experts * col_count * MOST)
    packed = packed.reshape(local_experts, col_count, MOST * features)
    arrived = lax.all_to_all(packed, "expert", split_axis=1, concat_axis=1, tiled=True)
    arrived = arrived.reshape(local_experts, col_count * MOST, features)
    both = jnp.einsum(
        "erd,egfd->gefr",
        lax.all_gather(arrived, "dp", axis=1, tiled=True),
        expert_in,
        preferred_element_type=jnp.float32,
    )
    hidden = (jax.nn.silu(both[0]) * both[1]).astype(jnp.bfloat16)
    piece = lax.all_gather(hidden, "dp", axis=1, tiled=True)
    width = piece.shape[1]
    blocks = piece.reshape(local_experts, width, dp_count, col_count, MOST)
    outputs = jnp.einsum(
        "efabm,efd->ebmad", blocks, expert_out, preferred_element_type=jnp.float32
    ).astype(jnp.bfloat16)
    outputs = outputs.reshape(local_experts, col_count, MOST, dp_count * slice_width)
    returned = lax.all_to_all(
        lax.all_to_all(outputs, "dp", split_axis=3, concat_axis=3, tiled=True),
        "expert",
        split_axis=1,
        concat_axis=1,
        tiled=True,
    )
    returned = returned.reshape(local_experts * col_count * MOST, features)
    picked = returned[own_slot].reshape(tok_count, route_count, features)
    mixed = jnp.sum(route_weight[:, :, None] * picked.astype(jnp.float32), axis=1)
    return mixed.astype(jnp.bfloat16)


def line_kernel(n, own_ref, out_ref, own_sem, send_sem, recv_sem):
    z, c = lax.axis_index("dp"), lax.axis_index("expert")
    barrier = pltpu.get_barrier_semaphore()

    @pl.when(z > 0)
    def _():
        pl.semaphore_signal(barrier, inc=1, device_id=(z - 1, c), device_id_type=MESH)

    @pl.when(z < n - 1)
    def _():
        pl.semaphore_signal(barrier, inc=1, device_id=(z + 1, c), device_id_type=MESH)

    own = pltpu.make_async_copy(own_ref, out_ref.at[z], own_sem)
    own.start()
    pl.semaphore_wait(barrier, (z > 0).astype(jnp.int32) + (z < n - 1).astype(jnp.int32))

    def copy(zz, way, target, first=False):
        return pltpu.make_async_remote_copy(
            src_ref=own_ref if first else out_ref.at[zz], dst_ref=out_ref.at[zz],
            send_sem=send_sem.at[zz, way], recv_sem=recv_sem.at[zz],
            device_id=(target, c), device_id_type=MESH,
        )

    @pl.when(z < n - 1)
    def _():
        copy(z, 0, z + 1, True).start()

    @pl.when(z > 0)
    def _():
        copy(z, 1, z - 1, True).start()

    for d in range(1, n):
        @pl.when(z - d >= 0)
        def _():
            copy(z - d, 0, (z + 1) % n).wait_recv()

            @pl.when(z < n - 1)
            def _():
                copy(z - d, 0, z + 1).start()

        @pl.when(z + d < n)
        def _():
            copy(z + d, 1, (z + 1) % n).wait_recv()

            @pl.when(z > 0)
            def _():
                copy(z + d, 1, z - 1).start()

    own.wait()
    for zz in range(n):
        @pl.when((z < n - 1) & (zz <= z))
        def _():
            copy(zz, 0, z + 1).wait_send()

        @pl.when((z > 0) & (zz >= z))
        def _():
            copy(zz, 1, z - 1).wait_send()


def expert_kernel(
    n, cols, groups, line_ref, place_ref, win_ref, wout_ref, perm_ref, weight_ref, out_ref,
    win, wout, tokens, pick, x, hid, outs, msg, got,
    win_sem, wout_sem, own_sem, tok_send, tok_recv, hid_send, hid_recv, msg_send, msg_recv,
):
    z, c = lax.axis_index("dp"), lax.axis_index("expert")
    me = z * cols + c
    total = n * cols
    experts, rows = win.shape[0], hid.shape[2]
    steps = groups * experts
    xn = c + 2 - 4 * ((c // 2) % 2)
    yn = c + 4 - 8 * (c // 4)
    diag = xn + 4 - 8 * (xn // 4)
    sib = c + 1 - 2 * (c % 2)
    half = tokens.shape[1] // 2
    features = win.shape[3]
    width = outs.shape[1]

    barrier = pltpu.get_barrier_semaphore()

    @pl.loop(1, total)
    def _(d):
        other = (me + d) % total
        pl.semaphore_signal(barrier, inc=1, device_id=(other // cols, other % cols), device_id_type=MESH)

    pl.semaphore_wait(barrier, total - 1)

    def own_block(zz):
        return pltpu.make_async_copy(line_ref.at[zz], tokens.at[zz * cols + c], own_sem.at[zz])

    def share(zz, col, kind, target, part=None):
        block = zz * cols + col
        dst, sem = tokens.at[block], tok_recv.at[block, 0]
        src = line_ref.at[zz] if kind < 3 else dst
        if part is not None:
            src = dst = tokens.at[block, pl.ds(part * half, half)]
            sem = tok_recv.at[block, part]
        return pltpu.make_async_remote_copy(
            src_ref=src, dst_ref=dst, send_sem=tok_send.at[block, kind], recv_sem=sem,
            device_id=(z, target), device_id_type=MESH,
        )

    def offer(zz):
        return [share(zz, c, 0, xn), share(zz, c, 1, yn), share(zz, c, 2, sib)]

    def relay(zz):
        return [
            share(zz, xn, 3, yn, 0), share(zz, xn, 4, sib),
            share(zz, yn, 3, xn, 1), share(zz, yn, 4, sib),
        ]

    def begin(zz):
        own_block(zz).start()
        for cp in offer(zz):
            cp.start()

    def forward(zz):
        share(zz, xn, 4, sib).wait_recv()
        for cp in relay(zz)[:2]:
            cp.start()
        share(zz, yn, 4, sib).wait_recv()
        for cp in relay(zz)[2:]:
            cp.start()

    def across(zz):
        share(zz, diag, 3, yn, 0).wait_recv()
        share(zz, diag, 3, xn, 1).wait_recv()
        share(zz, diag, 4, sib).start()

    def complete(zz):
        own_block(zz).wait()
        for col in (sib, xn + 1 - 2 * (xn % 2), yn + 1 - 2 * (yn % 2), diag + 1 - 2 * (diag % 2)):
            share(zz, col, 4, sib).wait_recv()

    per = n // groups
    for zz in range(per):
        begin(zz)
    @pl.loop(0, experts)
    def _(e):
        pltpu.make_async_copy(win_ref.at[e], win.at[e], win_sem.at[e]).start()

    @pl.loop(0, experts)
    def _(e):
        pltpu.make_async_copy(wout_ref.at[e], wout.at[e], wout_sem.at[e]).start()

    for zz in range(per, n):
        begin(zz)
    for zz in range(per):
        forward(zz)
    for zz in range(per):
        across(zz)
    for zz in range(per):
        complete(zz)

    def choose(g):
        size = tokens.shape[1] * per * cols
        for e in range(experts):
            at = lax.broadcasted_iota(jnp.int32, (rows, size), 0)
            named = place_ref[g, e:e + 1, :]
            pick[e * rows:(e + 1) * rows, :] = jnp.where(at == named, 1.0, 0.0).astype(jnp.bfloat16)

        @pl.loop(0, features // width)
        def _(j):
            at = pl.ds(pl.multiple_of(j * width, width), width)
            part = tokens[pl.ds(g * (per * cols), per * cols), :, at].reshape(size, width)
            x[:, at] = jnp.dot(pick[...], part, preferred_element_type=jnp.float32).astype(jnp.bfloat16)

    def pass_on(zz, e, way, target):
        return pltpu.make_async_remote_copy(
            src_ref=hid.at[zz, e], dst_ref=hid.at[zz, e], send_sem=hid_send.at[zz, e, way],
            recv_sem=hid_recv.at[zz, e], device_id=(target, c), device_id_type=MESH,
        )

    def upward(zz, e):
        @pl.when(z < n - 1)
        def _():
            pass_on(zz, e, 0, z + 1).start()

    def downward(zz, e):
        @pl.when(z > 0)
        def _():
            pass_on(zz, e, 1, z - 1).start()

    contract_last = (((1,), (1,)), ((), ()))

    choose(0)

    @pl.loop(0, steps + n - 1)
    def _(i):
        for g in range(1, groups):
            for k in range(per):
                @pl.when(i == (g - 1) * experts + 1 + 2 * k)
                def _():
                    forward(g * per + k)

                @pl.when(i == (g - 1) * experts + 3 + 2 * k)
                def _():
                    across(g * per + k)

            @pl.when(i == g * experts)
            def _():
                for k in range(per):
                    complete(g * per + k)
                choose(g)

        @pl.when(i < experts)
        def _():
            pltpu.make_async_copy(win_ref.at[i], win.at[i], win_sem.at[i]).wait()

        @pl.when(i < steps)
        def _():
            e = i % experts
            xe = x[pl.ds(pl.multiple_of(e * rows, rows), rows), :]
            gate = lax.dot_general(xe, win[e, 0], contract_last, preferred_element_type=jnp.float32)
            up = lax.dot_general(xe, win[e, 1], contract_last, preferred_element_type=jnp.float32)
            hid[z, i] = (gate / (1.0 + jnp.exp(-gate)) * up).astype(jnp.bfloat16)
            upward(z, i)
            downward(z, i)

        for d in range(1, n):
            e = i - d

            @pl.when((e >= 0) & (e < steps) & (z - d >= 0))
            def _():
                pass_on(z - d, e, 0, (z + 1) % n).wait_recv()
                upward(z - d, e)

            @pl.when((e >= 0) & (e < steps) & (z + d < n))
            def _():
                pass_on(z + d, e, 1, (z + 1) % n).wait_recv()
                downward(z + d, e)

        @pl.when(i >= n - 1)
        def _():
            step = i - (n - 1)
            e = step % experts

            @pl.when(step < experts)
            def _():
                pltpu.make_async_copy(wout_ref.at[e], wout.at[e], wout_sem.at[e]).wait()

            acc = jnp.zeros((rows, width), jnp.float32)
            for zz in range(n):
                acc += jnp.dot(hid[zz, step], wout[e, zz], preferred_element_type=jnp.float32)
            row = pl.multiple_of(step * rows, rows)
            outs[pl.ds(row, rows), :] = acc.astype(jnp.bfloat16)

    def message(dest):
        return pltpu.make_async_remote_copy(
            src_ref=msg.at[dest], dst_ref=got.at[me], send_sem=msg_send.at[dest],
            recv_sem=msg_recv.at[me], device_id=(dest // cols, dest % cols), device_id_type=MESH,
        )

    slots = msg.shape[1]

    @pl.loop(0, n)
    def _(j):
        zz = (z + 1 + j) % n
        part = perm_ref[pl.ds(pl.multiple_of(zz * (cols * slots), cols * slots), cols * slots), :]
        lanes = lax.broadcasted_iota(jnp.int32, (cols * slots, outs.shape[0]), 1)
        pick = jnp.where(lanes == part, 1.0, 0.0).astype(jnp.bfloat16)
        moved = jnp.dot(pick, outs[...], preferred_element_type=jnp.float32)
        msg[pl.ds(zz * cols, cols)] = moved.reshape(cols, slots, width).astype(jnp.bfloat16)

        @pl.loop(0, cols)
        def _(k):
            dest = zz * cols + (c + k) % cols

            @pl.when(dest != me)
            def _():
                message(dest).start()

    got[me] = msg[me]

    @pl.loop(1, total)
    def _(d):
        source = (me + d) % total
        pltpu.make_async_remote_copy(
            src_ref=msg.at[source], dst_ref=got.at[source], send_sem=msg_send.at[source],
            recv_sem=msg_recv.at[source], device_id=(source // cols, source % cols), device_id_type=MESH,
        ).wait_recv()

    tok = out_ref.shape[0]
    for zz in range(n):
        acc = jnp.zeros((2 * tok, width), jnp.float32)
        for col in range(cols):
            acc += jnp.dot(weight_ref[col], got[zz * cols + col], preferred_element_type=jnp.float32)
        out_ref[:, zz * width:(zz + 1) * width] = (acc[:tok] + acc[tok:]).astype(jnp.bfloat16)

    @pl.loop(1, total)
    def _(d):
        message((me + d) % total).wait_send()

    @pl.loop(0, n)
    def _(zz):
        for cp in offer(zz) + relay(zz) + [share(zz, diag, 4, sib)]:
            cp.wait_send()

    @pl.loop(0, steps)
    def _(e):
        for zz in range(n):
            @pl.when((z < n - 1) & (zz <= z))
            def _():
                pass_on(zz, e, 0, z + 1).wait_send()

            @pl.when((z > 0) & (zz >= z))
            def _():
                pass_on(zz, e, 1, z - 1).wait_send()


def fused(n, cols, tokens, routes, route_weight, expert_in, expert_out):
    tok, features = tokens.shape
    top = routes.shape[1]
    experts, _, hidden, _ = expert_in.shape
    width = expert_out.shape[2]
    total = n * cols
    col = lax.axis_index("expert")
    slots = experts * MOST
    rows = total * MOST

    chosen, rank = slot_parts(routes)
    rank = rank.reshape(tok, top)
    meta = jnp.concatenate([routes, rank], axis=1).reshape(1, tok * 2 * top)
    seen = lax.all_gather(meta, ("dp", "expert"), axis=0, tiled=True).reshape(total, tok, 2 * top)
    line = pl.pallas_call(
        functools.partial(line_kernel, n),
        out_shape=jax.ShapeDtypeStruct((n, tok, features), jnp.bfloat16),
        in_specs=[pl.BlockSpec(memory_space=pl.ANY)],
        out_specs=pl.BlockSpec(memory_space=pl.ANY),
        scratch_shapes=[
            pltpu.SemaphoreType.DMA,
            pltpu.SemaphoreType.DMA((n, 2)),
            pltpu.SemaphoreType.DMA((n,)),
        ],
        compiler_params=pltpu.CompilerParams(collective_id=0, has_side_effects=True),
    )(tokens)

    groups = 2
    per_group = rows // groups
    expert = col * experts + jnp.arange(experts, dtype=jnp.int32)
    base = (jnp.arange(total, dtype=jnp.int32) % (total // groups)) * MOST
    slot = seen[:, :, top:] + base[:, None, None] + 1
    match = seen[None, :, :, :top] == expert[:, None, None, None]
    place = jnp.sum(jnp.where(match, slot[None], 0), axis=3) - 1
    place = place.reshape(experts, groups, total // groups * tok).transpose(1, 0, 2)

    order = jnp.arange(total * slots, dtype=jnp.int32)
    dest = order // slots
    held = dest // (total // groups) * experts + order % slots // MOST
    perm = (held * per_group + dest % (total // groups) * MOST + order % MOST)[:, None]
    spot = (chosen * MOST).reshape(tok, top) + rank
    exact = jnp.sum(
        jnp.where(
            spot[:, :, None] == jnp.arange(cols * slots, dtype=jnp.int32), route_weight[:, :, None], 0.0
        ),
        axis=1,
    )
    high = lax.reduce_precision(exact, 8, 7)
    weight = jnp.concatenate([high, exact - high], axis=0).astype(jnp.bfloat16)
    weight = weight.reshape(2 * tok, cols, slots).transpose(1, 0, 2)

    vmem = pl.BlockSpec(memory_space=pltpu.VMEM)
    anywhere = pl.BlockSpec(memory_space=pl.ANY)
    return pl.pallas_call(
        functools.partial(expert_kernel, n, cols, groups),
        out_shape=jax.ShapeDtypeStruct((tok, features), jnp.bfloat16),
        in_specs=[anywhere, vmem, anywhere, anywhere, vmem, vmem],
        out_specs=vmem,
        scratch_shapes=[
            pltpu.VMEM((experts, 2, hidden, features), jnp.bfloat16),
            pltpu.VMEM((experts, n, hidden, width), jnp.bfloat16),
            pltpu.VMEM((total, tok, features), jnp.bfloat16),
            pltpu.VMEM((experts * per_group, total // groups * tok), jnp.bfloat16),
            pltpu.VMEM((experts * per_group, features), jnp.bfloat16),
            pltpu.VMEM((n, groups * experts, per_group, hidden), jnp.bfloat16),
            pltpu.VMEM((experts * rows, width), jnp.bfloat16),
            pltpu.VMEM((total, slots, width), jnp.bfloat16),
            pltpu.VMEM((total, slots, width), jnp.bfloat16),
            pltpu.SemaphoreType.DMA((experts,)),
            pltpu.SemaphoreType.DMA((experts,)),
            pltpu.SemaphoreType.DMA((n,)),
            pltpu.SemaphoreType.DMA((total, 5)),
            pltpu.SemaphoreType.DMA((total, 2)),
            pltpu.SemaphoreType.DMA((n, groups * experts, 2)),
            pltpu.SemaphoreType.DMA((n, groups * experts)),
            pltpu.SemaphoreType.DMA((total,)),
            pltpu.SemaphoreType.DMA((total,)),
        ],
        compiler_params=pltpu.CompilerParams(
            collective_id=1, has_side_effects=True, vmem_limit_bytes=63 * 1024 * 1024
        ),
    )(line, place, expert_in, expert_out.reshape(experts, n, hidden, width), perm, weight)


def solution(mesh):
    n, cols = mesh.shape["dp"], mesh.shape["expert"]

    def body(*args):
        if n * cols > 32 or cols != 8:
            return local(*args)
        return fused(n, cols, *args)

    return jax.shard_map(
        body,
        mesh=mesh,
        in_specs=(
            P(("dp", "expert"), None),
            P(("dp", "expert"), None),
            P(("dp", "expert"), None),
            P("expert", None, "dp", None),
            P("expert", None, "dp"),
        ),
        out_specs=P(("dp", "expert"), None),
        check_vma=False,
    )
```

time: 191 us -> 214 us (1.12)
  blocking collectives: 0 us -> 34 us
  matrix products: 11.6 us -> 0 us
  Pallas kernels: 166 us -> 169 us
    all_gather x0 -> x1, blocking collectives: none -> 34 us  [fused(): lax.all_gather(meta, ('dp', 'expert'), axis=0, tiled=True)]
    dot_general x1 -> x0, matrix products: 11.6 us -> none  [fused(): jnp.einsum('gst,gtd->gsd', pick.astype(jnp.bfloat16).reshape(groups, expe...]
    pallas_call x2, Pallas kernels: 166 us -> 169 us  [the longest x1 141 us: fused(): pl.pallas_call(functools.partial(expert_kernel, n, cols, groups), out_sha...]
where the time goes in v2:
time: 214 us; the launch traced here: 213 us
  Pallas kernels  169 us (79%)
  blocking collectives  34 us (16%)
  local copies, waits for them, and re-layouts  4.89 us (2%)
  other arithmetic  4.85 us (2%)
    pallas_call x1, Pallas kernels, fused(): pl.pallas_call(functools.partial(expert_kernel, n, cols, groups), out_sha...  141 us
    all_gather x1, blocking collectives, fused(): lax.all_gather(meta, ('dp', 'expert'), axis=0, tiled=True)  34 us
    pallas_call x1, Pallas kernels, fused(): pl.pallas_call(functools.partial(line_kernel, n), out_shape=jax.ShapeDtyp...  28 us

profile of v2, /device:TPU:25, one launch (start us, length us, event | category | flops | bytes accessed | tf_op | source)
XLA Modules:
  0.0 213.1 jit_solution(11029684822149183703)
XLA Ops:
  0.0 0.8 copy.42
  0.8 0.1 eq.47
  0.9 0.2 convert_reduce_fusion
  1.1 0.1 reshape.216
  1.2 0.1 pad_add_fusion
  1.3 0.1 copy.48
  1.3 0.1 reshape.220
  1.4 0.7 multiply_add_fusion
  2.1 34.0 %all-gather = s32[32,1,512]{2,1,0:T(1,128)S(1)} all-gather(s32[1,1,512]{2,1,0:T(1,128)S(1)} %reshape.220), channel_id=1, replica_groups=mesh['dp'=4,'expert'=8] {'dp','expert'}, dimensions={0}, use_global_device_ids=true | all-gather | bytes 67584 | tf_op jit(solution)/shard_map/all_gather | solution.py:392
  36.2 0.8 select_reduce_fusion.1
  37.0 0.1 copy.49
  37.2 0.1 pad_maximum_fusion
  37.3 0.9 copy.50
  38.1 0.1 copy.43
  38.3 0.1 copy.44
  38.4 0.1 copy.51
  38.5 0.1 add_add_fusion
  38.6 0.2 select_reduce_fusion
  38.7 0.1 sub.25
  38.8 0.6 copy.54
  39.5 2.7 %fusion.14.perm_ref = s32[1280,1]{1,0:T(8,128)} fusion(), kind=kLoop, calls=%fused_computation.25 | loop fusion | flops 65280 | bytes 5120 | tf_op jit(solution)/shard_map/add | solution.py:418
  42.2 28.0 %shard_map.55.line_ref = bf16[4,64,2048]{2,1,0:T(8,128)(2,1)} custom-call(bf16[64,2048]{1,0:T(8,128)(2,1)} %own_ref.1), custom_call_target="tpu_custom_call" | custom-call | tf_op jit(solution)/shard_map/pallas_call | solution.py:393
  70.2 141.2 %shard_map.56 = bf16[64,2048]{1,0:T(8,128)(2,1)} custom-call(bf16[4,64,2048]{2,1,0:T(8,128)(2,1)} %shard_map.55.line_ref, s32[2,8,1024]{2,1,0:T(8,128)} %bitcast.11, bf16[8,2,352,2048]{3,2,1,0:T(8,128)(2,1)} %win_ref.1, bf16[8,4,352,512]{3,2,1,0:T(8,128)(2,1)} %bitcast.7, s32[1280,1]{1,0:T(8,128)} %fusion.14.perm_ref, bf16[8,128,40]{2,1,0:T(8,128)(2,1)} %bitcast.8), custom_call_target="tpu_custom_call" | custom-call | tf_op jit(solution)/shard_map/pallas_call | solution.py:432
  211.5 1.7 copy.56
  (5 shorter events, 0.1 us)

commit v3 on v2

--- a/solution.py
+++ b/solution.py
@@ -8,6 +8,7 @@
 from jax.sharding import PartitionSpec as P
 
 MOST = 5
+LANES = 128
 MESH = pl.DeviceIdType.MESH
 
 
@@ -67,21 +68,30 @@
     return mixed.astype(jnp.bfloat16)
 
 
-def line_kernel(n, own_ref, out_ref, own_sem, send_sem, recv_sem):
+def line_kernel(
+    n, cols, own_ref, meta_ref, out_ref, metas_ref,
+    own_sem, send_sem, recv_sem, meta_sem, meta_send, meta_recv,
+):
     z, c = lax.axis_index("dp"), lax.axis_index("expert")
-    barrier = pltpu.get_barrier_semaphore()
-
-    @pl.when(z > 0)
-    def _():
-        pl.semaphore_signal(barrier, inc=1, device_id=(z - 1, c), device_id_type=MESH)
-
-    @pl.when(z < n - 1)
-    def _():
-        pl.semaphore_signal(barrier, inc=1, device_id=(z + 1, c), device_id_type=MESH)
-
+    me, total = z * cols + c, n * cols
     own = pltpu.make_async_copy(own_ref, out_ref.at[z], own_sem)
     own.start()
-    pl.semaphore_wait(barrier, (z > 0).astype(jnp.int32) + (z < n - 1).astype(jnp.int32))
+    own_meta = pltpu.make_async_copy(meta_ref, metas_ref.at[me], meta_sem)
+    own_meta.start()
+    barrier = pltpu.get_barrier_semaphore()
+
+    @pl.loop(1, total)
+    def _(d):
+        other = (me + d) % total
+        pl.semaphore_signal(barrier, inc=1, device_id=(other // cols, other % cols), device_id_type=MESH)
+
+    pl.semaphore_wait(barrier, total - 1)
+
+    def tell(other, slot):
+        return pltpu.make_async_remote_copy(
+            src_ref=meta_ref, dst_ref=metas_ref.at[slot], send_sem=meta_send.at[other],
+            recv_sem=meta_recv.at[slot], device_id=(other // cols, other % cols), device_id_type=MESH,
+        )
 
     def copy(zz, way, target, first=False):
         return pltpu.make_async_remote_copy(
@@ -98,6 +108,10 @@
     def _():
         copy(z, 1, z - 1, True).start()
 
+    @pl.loop(1, total)
+    def _(d):
+        tell((me + d) % total, me).start()
+
     for d in range(1, n):
         @pl.when(z - d >= 0)
         def _():
@@ -116,6 +130,14 @@
                 copy(z + d, 1, z - 1).start()
 
     own.wait()
+    own_meta.wait()
+
+    @pl.loop(1, total)
+    def _(d):
+        other = (me + d) % total
+        tell(other, other).wait_recv()
+        tell(other, me).wait_send()
+
     for zz in range(n):
         @pl.when((z < n - 1) & (zz <= z))
         def _():
@@ -251,6 +273,33 @@
 
     contract_last = (((1,), (1,)), ((), ()))
 
+    def message(dest):
+        return pltpu.make_async_remote_copy(
+            src_ref=msg.at[dest], dst_ref=got.at[me], send_sem=msg_send.at[dest],
+            recv_sem=msg_recv.at[me], device_id=(dest // cols, dest % cols), device_id_type=MESH,
+        )
+
+    slots = msg.shape[1]
+
+    def respond(g):
+        @pl.loop(0, per)
+        def _(j):
+            zz = g * per + j
+            part = perm_ref[pl.ds(pl.multiple_of(zz * (cols * slots), cols * slots), cols * slots), :]
+            lanes = lax.broadcasted_iota(jnp.int32, (cols * slots, experts * rows), 1)
+            take = jnp.where(lanes == part, 1.0, 0.0).astype(jnp.bfloat16)
+            held = outs[g * (experts * rows):(g + 1) * (experts * rows), :]
+            moved = jnp.dot(take, held, preferred_element_type=jnp.float32)
+            msg[pl.ds(zz * cols, cols)] = moved.reshape(cols, slots, width).astype(jnp.bfloat16)
+
+            @pl.loop(0, cols)
+            def _(k):
+                dest = zz * cols + (c + k) % cols
+
+                @pl.when(dest != me)
+                def _():
+                    message(dest).start()
+
     choose(0)
 
     @pl.loop(0, steps + n - 1)
@@ -313,31 +362,12 @@
             row = pl.multiple_of(step * rows, rows)
             outs[pl.ds(row, rows), :] = acc.astype(jnp.bfloat16)
 
-    def message(dest):
-        return pltpu.make_async_remote_copy(
-            src_ref=msg.at[dest], dst_ref=got.at[me], send_sem=msg_send.at[dest],
-            recv_sem=msg_recv.at[me], device_id=(dest // cols, dest % cols), device_id_type=MESH,
-        )
-
-    slots = msg.shape[1]
-
-    @pl.loop(0, n)
-    def _(j):
-        zz = (z + 1 + j) % n
-        part = perm_ref[pl.ds(pl.multiple_of(zz * (cols * slots), cols * slots), cols * slots), :]
-        lanes = lax.broadcasted_iota(jnp.int32, (cols * slots, outs.shape[0]), 1)
-        pick = jnp.where(lanes == part, 1.0, 0.0).astype(jnp.bfloat16)
-        moved = jnp.dot(pick, outs[...], preferred_element_type=jnp.float32)
-        msg[pl.ds(zz * cols, cols)] = moved.reshape(cols, slots, width).astype(jnp.bfloat16)
-
-        @pl.loop(0, cols)
-        def _(k):
-            dest = zz * cols + (c + k) % cols
-
-            @pl.when(dest != me)
-            def _():
-                message(dest).start()
-
+        for g in range(groups - 1):
+            @pl.when(i == (g + 1) * experts + n - 2)
+            def _():
+                respond(g)
+
+    respond(groups - 1)
     got[me] = msg[me]
 
     @pl.loop(1, total)
@@ -388,20 +418,28 @@
 
     chosen, rank = slot_parts(routes)
     rank = rank.reshape(tok, top)
-    meta = jnp.concatenate([routes, rank], axis=1).reshape(1, tok * 2 * top)
-    seen = lax.all_gather(meta, ("dp", "expert"), axis=0, tiled=True).reshape(total, tok, 2 * top)
-    line = pl.pallas_call(
-        functools.partial(line_kernel, n),
-        out_shape=jax.ShapeDtypeStruct((n, tok, features), jnp.bfloat16),
-        in_specs=[pl.BlockSpec(memory_space=pl.ANY)],
-        out_specs=pl.BlockSpec(memory_space=pl.ANY),
+    meta = jnp.concatenate([routes, rank], axis=1).reshape(-1, LANES)
+    filled = meta.shape[0]
+    meta = jnp.pad(meta, ((0, -filled % 8), (0, 0)))
+    line, metas = pl.pallas_call(
+        functools.partial(line_kernel, n, cols),
+        out_shape=[
+            jax.ShapeDtypeStruct((n, tok, features), jnp.bfloat16),
+            jax.ShapeDtypeStruct((total,) + meta.shape, jnp.int32),
+        ],
+        in_specs=[pl.BlockSpec(memory_space=pl.ANY)] * 2,
+        out_specs=[pl.BlockSpec(memory_space=pl.ANY)] * 2,
         scratch_shapes=[
             pltpu.SemaphoreType.DMA,
             pltpu.SemaphoreType.DMA((n, 2)),
             pltpu.SemaphoreType.DMA((n,)),
+            pltpu.SemaphoreType.DMA,
+            pltpu.SemaphoreType.DMA((total,)),
+            pltpu.SemaphoreType.DMA((total,)),
         ],
         compiler_params=pltpu.CompilerParams(collective_id=0, has_side_effects=True),
-    )(tokens)
+    )(tokens, meta)
+    seen = metas[:, :filled].reshape(total, tok, 2 * top)
 
     groups = 2
     per_group = rows // groups
@@ -414,7 +452,7 @@
 
     order = jnp.arange(total * slots, dtype=jnp.int32)
     dest = order // slots
-    held = dest // (total // groups) * experts + order % slots // MOST
+    held = order % slots // MOST
     perm = (held * per_group + dest % (total // groups) * MOST + order % MOST)[:, None]
     spot = (chosen * MOST).reshape(tok, top) + rank
     exact = jnp.sum(

time: 214 us -> 201 us (0.939)
  blocking collectives: 34 us -> 0 us
  Pallas kernels: 169 us -> 190 us
    all_gather x1 -> x0, blocking collectives: 34 us -> none  [fused(): lax.all_gather(meta, ('dp', 'expert'), axis=0, tiled=True)]
    pallas_call x1, Pallas kernels: 141 us -> 163 us  [fused(): pl.pallas_call(functools.partial(expert_kernel, n, cols, groups), out_sha...]
where the time goes in v3:
time: 201 us
  Pallas kernels  190 us (95%)
  local copies, waits for them, and re-layouts  6.39 us (3%)
  other arithmetic  4.49 us (2%)
    pallas_call x1, Pallas kernels, fused(): pl.pallas_call(functools.partial(expert_kernel, n, cols, groups), out_sha...  163 us
    pallas_call x1, Pallas kernels, fused(): pl.pallas_call(functools.partial(line_kernel, n, cols), out_shape=[jax.Sh...  26.8 us

profile of v3, /device:TPU:25, one launch (start us, length us, event | category | flops | bytes accessed | tf_op | source)
XLA Modules:
  0.0 201.0 jit_solution(17225039320920524612)
XLA Ops:
  0.0 0.8 copy.43
  0.8 0.1 eq.47
  0.9 0.2 convert_reduce_fusion
  1.1 0.1 reshape.179
  1.2 0.1 pad_add_fusion
  1.3 0.1 reshape.180
  1.4 0.6 pad.4.meta_ref
  2.0 26.8 %shard_map.55 = (bf16[4,64,2048]{2,1,0:T(8,128)(2,1)}, s32[32,8,128]{2,1,0:T(8,128)}) custom-call(bf16[64,2048]{1,0:T(8,128)(2,1)} %own_ref.1, s32[8,128]{1,0:T(8,128)} %pad.4.meta_ref), custom_call_target="tpu_custom_call" | custom-call | tf_op jit(solution)/shard_map/pallas_call | solution.py:424
  28.8 0.9 slice.9
  29.7 0.1 copy.44
  29.9 0.1 copy.51
  30.0 0.1 add_add_fusion
  30.1 0.1 copy.45
  30.2 0.1 select_reduce_fusion
  30.4 0.1 sub.21
  30.5 0.6 copy.53
  31.1 0.1 copy.48
  31.2 0.7 multiply_add_fusion
  31.9 0.8 select_reduce_fusion.1
  32.7 0.1 copy.49
  32.9 0.1 pad_maximum_fusion
  33.0 0.9 copy.50
  33.8 2.3 %fusion.12.perm_ref = s32[1280,1]{1,0:T(8,128)} fusion(), kind=kLoop, calls=%fused_computation.21 | loop fusion | flops 52480 | bytes 5120 | tf_op jit(solution)/shard_map/add | solution.py:456
  36.1 163.2 %shard_map.56 = bf16[64,2048]{1,0:T(8,128)(2,1)} custom-call(bf16[4,64,2048]{2,1,0:T(8,128)(2,1)} %get-tuple-element.7.line_ref, s32[2,8,1024]{2,1,0:T(8,128)} %bitcast.11, bf16[8,2,352,2048]{3,2,1,0:T(8,128)(2,1)} %win_ref.1, bf16[8,4,352,512]{3,2,1,0:T(8,128)(2,1)} %bitcast.7, s32[1280,1]{1,0:T(8,128)} %fusion.12.perm_ref, bf16[8,128,40]{2,1,0:T(8,128)(2,1)} %bitcast.8), custom_call_target="tpu_custom_call" | custom-call | tf_op jit(solution)/shard_map/pallas_call | solution.py:470
  199.3 1.7 copy.55
  (5 shorter events, 0.1 us)

commit v4 on v3

--- a/solution.py
+++ b/solution.py
@@ -362,12 +362,8 @@
             row = pl.multiple_of(step * rows, rows)
             outs[pl.ds(row, rows), :] = acc.astype(jnp.bfloat16)
 
-        for g in range(groups - 1):
-            @pl.when(i == (g + 1) * experts + n - 2)
-            def _():
-                respond(g)
-
-    respond(groups - 1)
+    for g in range(groups):
+        respond(g)
     got[me] = msg[me]
 
     @pl.loop(1, total)

time: 201 us -> 181 us (0.900)
  Pallas kernels: 190 us -> 169 us
    pallas_call x1, Pallas kernels: 163 us -> 143 us  [fused(): pl.pallas_call(functools.partial(expert_kernel, n, cols, groups), out_sha...]
where the time goes in v4:
time: 181 us; the launch traced here: 180 us
  Pallas kernels  169 us (93%)
  local copies, waits for them, and re-layouts  6.39 us (4%)
  other arithmetic  4.49 us (2%)
    pallas_call x1, Pallas kernels, fused(): pl.pallas_call(functools.partial(expert_kernel, n, cols, groups), out_sha...  143 us
    pallas_call x1, Pallas kernels, fused(): pl.pallas_call(functools.partial(line_kernel, n, cols), out_shape=[jax.Sh...  26.8 us

profile of v4, /device:TPU:25, one launch (start us, length us, event | category | flops | bytes accessed | tf_op | source)
XLA Modules:
  0.0 180.4 jit_solution(18438536924365400858)
XLA Ops:
  0.0 0.8 copy.43
  0.8 0.1 eq.47
  0.9 0.2 convert_reduce_fusion
  1.1 0.1 reshape.179
  1.2 0.1 pad_add_fusion
  1.3 0.1 reshape.180
  1.4 0.6 pad.4.meta_ref
  2.0 26.8 %shard_map.55 = (bf16[4,64,2048]{2,1,0:T(8,128)(2,1)}, s32[32,8,128]{2,1,0:T(8,128)}) custom-call(bf16[64,2048]{1,0:T(8,128)(2,1)} %own_ref.1, s32[8,128]{1,0:T(8,128)} %pad.4.meta_ref), custom_call_target="tpu_custom_call" | custom-call | tf_op jit(solution)/shard_map/pallas_call | solution.py:420
  28.8 0.9 slice.9
  29.7 0.1 copy.44
  29.9 0.1 copy.51
  30.0 0.1 add_add_fusion
  30.1 0.1 copy.45
  30.2 0.1 select_reduce_fusion
  30.4 0.1 sub.21
  30.5 0.6 copy.53
  31.1 0.1 copy.48
  31.2 0.7 multiply_add_fusion
  31.9 0.8 select_reduce_fusion.1
  32.7 0.1 copy.49
  32.9 0.1 pad_maximum_fusion
  33.0 0.9 copy.50
  33.8 2.3 %fusion.12.perm_ref = s32[1280,1]{1,0:T(8,128)} fusion(), kind=kLoop, calls=%fused_computation.21 | loop fusion | flops 52480 | bytes 5120 | tf_op jit(solution)/shard_map/add | solution.py:452
  36.1 142.6 %shard_map.56 = bf16[64,2048]{1,0:T(8,128)(2,1)} custom-call(bf16[4,64,2048]{2,1,0:T(8,128)(2,1)} %get-tuple-element.7.line_ref, s32[2,8,1024]{2,1,0:T(8,128)} %bitcast.11, bf16[8,2,352,2048]{3,2,1,0:T(8,128)(2,1)} %win_ref.1, bf16[8,4,352,512]{3,2,1,0:T(8,128)(2,1)} %bitcast.7, s32[1280,1]{1,0:T(8,128)} %fusion.12.perm_ref, bf16[8,128,40]{2,1,0:T(8,128)(2,1)} %bitcast.8), custom_call_target="tpu_custom_call" | custom-call | tf_op jit(solution)/shard_map/pallas_call | solution.py:466
  178.7 1.7 copy.55
  (5 shorter events, 0.1 us)
